TPU v7x, 32 devices: a whole 2x2x4 slice. The times are simulated.
32 devices in a mesh: fsdp: 32 (over z, y, x, core).
Axes of the slice: x: 2, y: 2, z: 4, core: 2. Of those that a mesh axis runs over, the one named last changes fastest.
Arguments:
- tokens: bfloat16 [16384, 1024], P('fsdp'), may hold values from -6 to 6
- segment_ids: int32 [16384], P('fsdp'), may hold values from -1 to 3, as said below
- cotangent: bfloat16 [16384, 1024], P('fsdp'), may hold values from -6 to 6
- w_qkv: bfloat16 [1024, 3072], P('fsdp'), may hold values from -0.1875 to 0.1875
- w_out: bfloat16 [1024, 1024], P('fsdp'), may hold values from -0.75 to 0.75
- w_up: bfloat16 [1024, 4096], P('fsdp'), may hold values from -0.1875 to 0.1875
- w_down: bfloat16 [4096, 1024], P('fsdp'), may hold values from -0.09375 to 0.09375
- b_qkv: bfloat16 [3072], P('fsdp'), may hold values from -1.5 to 1.5
- b_out: bfloat16 [1024], P('fsdp'), may hold values from -1.5 to 1.5
- b_up: bfloat16 [4096], P('fsdp'), may hold values from -1.5 to 1.5
- b_down: bfloat16 [1024], P('fsdp'), may hold values from -1.5 to 1.5
- gain_attn: bfloat16 [1024], P('fsdp'), may hold values from 0.5 to 1.5
- shift_attn: bfloat16 [1024], P('fsdp'), may hold values from -1.5 to 1.5
- gain_mlp: bfloat16 [1024], P('fsdp'), may hold values from 0.5 to 1.5
- shift_mlp: bfloat16 [1024], P('fsdp'), may hold values from -1.5 to 1.5
Outputs:
- layer_out: bfloat16 [16384, 1024], P('fsdp')
- tokens_grad: float32 [16384, 1024], P('fsdp')
- grad_w_qkv: float32 [1024, 3072], P('fsdp')
- grad_w_out: float32 [1024, 1024], P('fsdp')
- grad_w_up: float32 [1024, 4096], P('fsdp')
- grad_w_down: float32 [4096, 1024], P('fsdp')
- grad_b_qkv: float32 [3072], P('fsdp')
- grad_b_out: float32 [1024], P('fsdp')
- grad_b_up: float32 [4096], P('fsdp')
- grad_b_down: float32 [1024], P('fsdp')
- grad_gain_attn: float32 [1024], P('fsdp')
- grad_shift_attn: float32 [1024], P('fsdp')
- grad_gain_mlp: float32 [1024], P('fsdp')
- grad_shift_mlp: float32 [1024], P('fsdp')
Inputs may be any that keep to these rules, and one draw needn't show every extreme that they name: `segment_ids`: each device's 512 slots form blocks of 128; a sequence starts at a block's first slot and covers whole consecutive blocks of one device; its live slots are a prefix and the rest of its last block is padding marked -1; live slots carry the sequence's number on its device, counted from 0 in order of slots.
All inputs are finite; a program needn't handle non-finite values.
Results may differ from a plain program's by a relative error of at most 0.0095.
Values may be sent and summed in bfloat16 or wider, within the bound.
No kernel may reach another device: no remote copies, remote signals or barrier semaphores. Data moves between devices by JAX's collectives and lax.ppermute only.
A program may use at most 256 MiB of HBM per device.

v0:
```python
from functools import partial

import jax
import jax.numpy as jnp
from jax import lax
from jax.sharding import PartitionSpec as P

D = 1024
HEADS = 16
HEAD_DIM = 64
ROTARY = 16


epsilon = 1e-05


def rotary_tables(position):
    inv_freq = 10000.0 ** (-jnp.arange(ROTARY // 2, dtype=jnp.float32) * 2.0 / ROTARY)
    angles = position[:, None] * inv_freq[None, :]
    return (jnp.cos(angles)[:, None, :], jnp.sin(angles)[:, None, :])


def rotate(features, cos_table, sin_table):
    half_dims = ROTARY // 2
    lower_half = features[..., :half_dims]
    upper_half = features[..., half_dims:ROTARY]
    return jnp.concatenate(
        [
            lower_half * cos_table - upper_half * sin_table,
            upper_half * cos_table + lower_half * sin_table,
            features[..., ROTARY:],
        ],
        axis=-1,
    )


def allowed_mask(seg_rows, seg_cols, row_index, col_index):
    same_seq = (
        (seg_rows[:, None] == seg_cols[None, :])
        & (seg_cols[None, :] >= 0)
        & (col_index[None, :] <= row_index[:, None])
    )
    return same_seq | (col_index[None, :] == row_index[:, None])


def inner_rows(left_side, right_side):
    return lax.dot_general(
        left_side, right_side, (((0,), (0,)), ((), ())), preferred_element_type=jnp.float32
    )


def times_transpose(left_side, right_side):
    return lax.dot_general(
        left_side, right_side, (((1,), (1,)), ((), ())), preferred_element_type=jnp.float32
    )


def block_scores(query_block, key_part, segment_ids, tok_index):
    raw_scores = jnp.einsum(
        "qhd,khd->hqk", query_block, key_part, preferred_element_type=jnp.float32
    ) * HEAD_DIM ** (-0.5)
    allowed = allowed_mask(segment_ids, segment_ids, tok_index, tok_index)
    return jnp.where(allowed[None], raw_scores, -1e30)


def column_sums(values):
    return jnp.sum(values.astype(jnp.float32), axis=0)


def on_device(
    tokens,
    segment_ids,
    cotangent,
    w_qkv,
    w_out,
    w_up,
    w_down,
    b_qkv,
    b_out,
    b_up,
    b_down,
    gain_attn,
    shift_attn,
    gain_mlp,
    shift_mlp,
):
    gathered = (
        lax.all_gather(w_qkv, "fsdp", axis=0, tiled=True),
        lax.all_gather(w_out, "fsdp", axis=0, tiled=True),
        lax.all_gather(w_up, "fsdp", axis=0, tiled=True),
        lax.all_gather(w_down, "fsdp", axis=0, tiled=True),
        lax.all_gather(b_qkv, "fsdp", axis=0, tiled=True),
        lax.all_gather(b_out, "fsdp", axis=0, tiled=True),
        lax.all_gather(b_up, "fsdp", axis=0, tiled=True),
        lax.all_gather(b_down, "fsdp", axis=0, tiled=True),
        lax.all_gather(gain_attn, "fsdp", axis=0, tiled=True),
        lax.all_gather(shift_attn, "fsdp", axis=0, tiled=True),
        lax.all_gather(gain_mlp, "fsdp", axis=0, tiled=True),
        lax.all_gather(shift_mlp, "fsdp", axis=0, tiled=True),
    )
    wqkv_all, wout_all, wup_all, wdown_all = (gathered[0], gathered[1], gathered[2], gathered[3])
    bias_qkv = gathered[4].astype(jnp.float32)
    bias_out = gathered[5].astype(jnp.float32)
    bias_up = gathered[6].astype(jnp.float32)
    bias_down = gathered[7].astype(jnp.float32)
    gain_one = gathered[8].astype(jnp.float32)
    shift_one = gathered[9].astype(jnp.float32)
    gain_two = gathered[10].astype(jnp.float32)
    shift_two = gathered[11].astype(jnp.float32)
    tok_count = tokens.shape[0]
    tok_index = jnp.arange(tok_count, dtype=jnp.int32)
    same_seq = segment_ids[:, None] == segment_ids[None, :]
    seq_start = jnp.min(jnp.where(same_seq, tok_index[None, :], tok_count), axis=1)
    position = (tok_index - seq_start).astype(jnp.float32)
    cos_table, sin_table = rotary_tables(position)
    inputs = tokens.astype(jnp.float32)
    center = inputs - jnp.mean(inputs, axis=-1, keepdims=True)
    inv_scale = lax.rsqrt(jnp.mean(center * center, axis=-1, keepdims=True) + epsilon)
    normed = center * inv_scale
    h_attn = (normed * gain_one + shift_one).astype(jnp.bfloat16)
    h_mlp = (normed * gain_two + shift_two).astype(jnp.bfloat16)
    joined = jnp.dot(h_attn, wqkv_all, preferred_element_type=jnp.float32) + bias_qkv
    query_rot = rotate(
        joined[:, :D].reshape(tok_count, HEADS, HEAD_DIM), cos_table, sin_table
    ).astype(jnp.bfloat16)
    key_rot = rotate(
        joined[:, D : 2 * D].reshape(tok_count, HEADS, HEAD_DIM), cos_table, sin_table
    ).astype(jnp.bfloat16)
    value_low = joined[:, 2 * D :].reshape(tok_count, HEADS, HEAD_DIM).astype(jnp.bfloat16)
    block_rows = min(512, tok_count)
    scores = block_scores(query_rot, key_rot, segment_ids, tok_index)
    row_max = jnp.max(scores, axis=-1, keepdims=True)
    weights = jnp.exp(scores - row_max)
    row_sum = jnp.sum(weights, axis=-1, keepdims=True)
    attn_prob = (weights / row_sum).astype(jnp.bfloat16)
    attended_blocks = jnp.einsum(
        "hqk,khd->qhd", attn_prob, value_low, preferred_element_type=jnp.float32
    )
    attended = attended_blocks.reshape(tok_count, D).astype(jnp.bfloat16)
    branch_attn = jnp.dot(attended, wout_all, preferred_element_type=jnp.float32) + bias_out
    pre_up = jnp.dot(h_mlp, wup_all, preferred_element_type=jnp.float32) + bias_up
    gelu_value, gelu_pull = jax.vjp(partial(jax.nn.gelu, approximate=False), pre_up)
    hidden = gelu_value.astype(jnp.bfloat16)
    branch_mlp = jnp.dot(hidden, wdown_all, preferred_element_type=jnp.float32) + bias_down
    layer_out = (inputs + branch_attn + branch_mlp).astype(jnp.bfloat16)
    again = (
        lax.all_gather(w_qkv, "fsdp", axis=0, tiled=True),
        lax.all_gather(w_out, "fsdp", axis=0, tiled=True),
        lax.all_gather(w_up, "fsdp", axis=0, tiled=True),
        lax.all_gather(w_down, "fsdp", axis=0, tiled=True),
        lax.all_gather(gain_attn, "fsdp", axis=0, tiled=True),
        lax.all_gather(gain_mlp, "fsdp", axis=0, tiled=True),
    )
    wqkv_bwd, wout_bwd, wup_bwd, wdown_bwd = (again[0], again[1], again[2], again[3])
    gain_one_bwd = again[4].astype(jnp.float32)
    gain_two_bwd = again[5].astype(jnp.float32)
    live_rows = (segment_ids >= 0).astype(jnp.float32)
    grad_out = cotangent.astype(jnp.float32) * live_rows[:, None]
    grad_low = grad_out.astype(jnp.bfloat16)
    grad_bias_out = column_sums(grad_low)
    grad_wout = inner_rows(attended, grad_low)
    grad_wdown = inner_rows(hidden, grad_low)
    d_hidden = times_transpose(grad_low, wdown_bwd)
    d_pre = gelu_pull(d_hidden)[0].astype(jnp.bfloat16)
    grad_bias_up = column_sums(d_pre)
    grad_wup = inner_rows(h_mlp, d_pre)
    d_h_mlp = times_transpose(d_pre, wup_bwd)
    grad_gain_mlp = jnp.sum(d_h_mlp * normed, axis=0)
    grad_shift_mlp = jnp.sum(d_h_mlp, axis=0)
    d_att = (
        times_transpose(grad_low, wout_bwd).astype(jnp.bfloat16).reshape(tok_count, HEADS, HEAD_DIM)
    )
    key_grad = jnp.zeros((tok_count, HEADS, HEAD_DIM), jnp.float32)
    value_grad = jnp.zeros((tok_count, HEADS, HEAD_DIM), jnp.float32)
    scores = block_scores(query_rot, key_rot, segment_ids, tok_index)
    attn_prob = jnp.exp(scores - row_max) / row_sum
    d_prob = jnp.einsum("qhd,khd->hqk", d_att, value_low, preferred_element_type=jnp.float32)
    row_dot = jnp.sum(attn_prob * d_prob, axis=-1, keepdims=True)
    d_score = (attn_prob * (d_prob - row_dot)).astype(jnp.bfloat16)
    query_grads = jnp.einsum(
        "hqk,khd->qhd", d_score, key_rot, preferred_element_type=jnp.float32
    ) * HEAD_DIM ** (-0.5)
    key_grad = key_grad.at[:block_rows].add(
        jnp.einsum("hqk,qhd->khd", d_score, query_rot, preferred_element_type=jnp.float32)
        * HEAD_DIM ** (-0.5)
    )
    value_grad = value_grad.at[:block_rows].add(
        jnp.einsum(
            "hqk,qhd->khd",
            attn_prob.astype(jnp.bfloat16),
            d_att,
            preferred_element_type=jnp.float32,
        )
    )
    query_grad = rotate(query_grads, cos_table, -sin_table)
    key_grad = rotate(key_grad, cos_table, -sin_table)
    d_joined = jnp.concatenate(
        [
            query_grad.reshape(tok_count, D),
            key_grad.reshape(tok_count, D),
            value_grad.reshape(tok_count, D),
        ],
        axis=1,
    ).astype(jnp.bfloat16)
    grad_bias_qkv = column_sums(d_joined)
    grad_wqkv = inner_rows(h_attn, d_joined)
    d_h_attn = times_transpose(d_joined, wqkv_bwd)
    grad_gain_attn = jnp.sum(d_h_attn * normed, axis=0)
    grad_shift_attn = jnp.sum(d_h_attn, axis=0)
    d_norm = d_h_attn * gain_one_bwd + d_h_mlp * gain_two_bwd
    d_inner = (
        d_norm
        - jnp.mean(d_norm, axis=-1, keepdims=True)
        - normed * jnp.mean(d_norm * normed, axis=-1, keepdims=True)
    )
    tokens_grad = grad_out + d_inner * inv_scale
    all_sums = (
        lax.psum_scatter(grad_wqkv, "fsdp", scatter_dimension=0, tiled=True),
        lax.psum_scatter(grad_wout, "fsdp", scatter_dimension=0, tiled=True),
        lax.psum_scatter(grad_wup, "fsdp", scatter_dimension=0, tiled=True),
        lax.psum_scatter(grad_wdown, "fsdp", scatter_dimension=0, tiled=True),
        lax.psum_scatter(grad_bias_qkv, "fsdp", scatter_dimension=0, tiled=True),
        lax.psum_scatter(grad_bias_out, "fsdp", scatter_dimension=0, tiled=True),
        lax.psum_scatter(grad_bias_up, "fsdp", scatter_dimension=0, tiled=True),
        lax.psum_scatter(grad_gain_attn, "fsdp", scatter_dimension=0, tiled=True),
        lax.psum_scatter(grad_shift_attn, "fsdp", scatter_dimension=0, tiled=True),
        lax.psum_scatter(grad_gain_mlp, "fsdp", scatter_dimension=0, tiled=True),
        lax.psum_scatter(grad_shift_mlp, "fsdp", scatter_dimension=0, tiled=True),
    )
    return (
        layer_out,
        tokens_grad,
        all_sums[0],
        all_sums[1],
        all_sums[2],
        all_sums[3],
        all_sums[4],
        all_sums[5],
        all_sums[6],
        all_sums[5],
        all_sums[7],
        all_sums[8],
        all_sums[9],
        all_sums[10],
    )


def solution(mesh):
    in_specs = (
        P("fsdp", None),
        P("fsdp"),
        P("fsdp", None),
        P("fsdp", None),
        P("fsdp", None),
        P("fsdp", None),
        P("fsdp", None),
        P("fsdp"),
        P("fsdp"),
        P("fsdp"),
        P("fsdp"),
        P("fsdp"),
        P("fsdp"),
        P("fsdp"),
        P("fsdp"),
    )
    out_specs = (
        P("fsdp", None),
        P("fsdp", None),
        P("fsdp", None),
        P("fsdp", None),
        P("fsdp", None),
        P("fsdp", None),
        P("fsdp"),
        P("fsdp"),
        P("fsdp"),
        P("fsdp"),
        P("fsdp"),
        P("fsdp"),
        P("fsdp"),
        P("fsdp"),
    )
    return jax.shard_map(
        on_device, mesh=mesh, in_specs=in_specs, out_specs=out_specs, check_vma=False
    )
```

profile of v0, /device:TPU:14, one launch (start us, length us, event | category | flops | bytes accessed | tf_op | source)
XLA Modules:
  0.0 979.8 jit_solution(2995277201870499112)
XLA Ops:
  7.2 0.7 all-gather.8.cloned.1.call-update
  8.0 0.7 all-gather.6.cloned.1.call-update
  8.7 0.7 all-gather.10.cloned.1.call-update
  10.1 0.8 dynamic-update-slice.10
  10.9 0.8 dynamic-update-slice.4
  11.7 0.8 dynamic-update-slice.5
  12.6 0.8 dynamic-update-slice.7
  13.4 0.8 dynamic-update-slice.8
  14.2 0.8 dynamic-update-slice.9
  15.1 0.8 dynamic-update-slice.6
  15.9 41.4 %all-reduce.15 = (bf16[1024]{0:T(1024)(128)(2,1)}, bf16[1024]{0:T(1024)(128)(2,1)}, bf16[3072]{0:T(1024)(128)(2,1)S(1)}, bf16[1024]{0:T(1024)(128)(2,1)S(1)}, bf...) all-reduce(bf16[1024]{0:T(1024)(128)(2,1)S(1)} %dynamic-update-slic, ...), channel_id=1, replica_groups=mesh['fsdp'=32] {'fsdp'}, use_global_device_ids=true, to_apply=%add.5 | all-reduce | flops 9216 | bytes 36864
  57.4 1.0 fusion.45
  58.4 1.4 convert_reduce_fusion.2
  59.8 1.6 fusion.33
  61.5 0.7 fusion.71
  62.3 1.7 fusion.47
  64.0 2.9 all-gather.8.cloned.1.call-done
  66.9 3.2 convolution_convert_fusion
  70.1 1.3 copy.55
  71.5 67.5 %all-gather.6.cloned.1.call-done = bf16[1024,3072]{1,0:T(8,128)(2,1)} async-done(((bf16[32,3072]{1,0:T(8,128)(2,1)}), bf16[1024,3072]{1,0:T(8,128)(2,1)}) %all-gather.6.cloned.1.call-update) | async-done | bytes 6291472 | tf_op jit(solution)/shard_map/all_gather | solution.py:88
  138.9 5.7 convolution_add_fusion
  144.8 1.8 fusion.73
  146.6 2.9 copy.52
  149.5 1.8 copy.53
  151.3 1.5 slice.142
  152.9 1.8 slice.143
  154.7 1.3 copy.51
  156.0 1.3 subtract_convert_fusion.3
  157.4 10.6 %fusion.74 = (f32[16,512]{1,0:T(8,128)S(1)}, f32[16,512,512]{1,2,0:T(8,128)}) fusion(pred[512,512]{0,1:T(8,128)(4,1)} %fusion.47, bf16[512,16,48]{0,2,1:T(8,128)(2,1)S(1)} %slice.142, bf16[512,16,8]{0,2,1:T(8,128)(2,1)S(1)} %get-tuple-element.98, bf16[512,16,8]{0,2,1:T(8,128)(2,1)S(1)} %get-tuple-element.99, bf16[512,16,48]{0,2,1:T(8,128)(2,1)S(1)} %slice.143, ...), kind=kOutput, calls=%fused_computation.117 | convolution fusion | flops 559940096 | bytes 19169280 | tf_op jit(solution)/shard_map/sub | solution.py:133
  168.1 7.5 fusion.39
  175.5 1.0 copy-done.18
  176.5 3.4 fusion.61
  180.2 14.3 %multiply_reduce_fusion = (f32[16,512]{1,0:T(8,128)}, f32[16,512,512]{1,2,0:T(8,128)}) fusion(f32[16,512,512]{1,2,0:T(8,128)} %get-tuple-element.105, f32[16,512]{1,0:T(8,128)S(1)} %get-tuple-element.104, bf16[512,16,64]{0,2,1:T(8,128)(2,1)} %bitcast.50, bf16[512,16,64]{0,2,1:T(8,128)(2,1)} %bitcast.55), kind=kOutput, calls=%fused_computation.2 | convolution fusion | flops 549445632 | bytes 35717120 | tf_op jit(solution)/shard_map/qhd,khd->hqk/dot_general | solution.py:177
  195.0 1.2 slice-done.2
  196.2 1.3 slice-done.3
  197.5 8.2 multiply_convert_fusion
  205.7 5.2 multiply_bitcast_fusion
  210.9 1.5 slice.140
  212.4 2.6 multiply_bitcast_fusion.1
  215.2 1.2 subtract_convert_fusion.1
  216.4 1.6 pad_maximum_fusion.3
  217.9 4.8 fusion.42
  222.8 10.4 %fusion.55 = f32[1024,3072]{1,0:T(8,128)} fusion(bf16[512,1024]{1,0:T(8,128)(2,1)} %param.23, f32[1024]{0:T(1024)S(1)} %copy-done.11, f32[1024]{0:T(1024)S(1)} %convert_element_type.96, f32[512]{0:T(512)S(1)} %add_rsqrt_fusion, f32[512]{0:T(512)S(1)} %broadcast_multiply_fusion.2, bf16[512,1024]{0,1:T(8,128)(2,1)} %bitcast.52, ...), kind=kOutput, calls=%fused_computation.107 | convolution fusion | flops 3233808384 | bytes 16789504 | tf_op jit(solution)/shard_map/dot_general | solution.py:47
  233.9 29.3 %all-gather = bf16[32,1,128]{2,1,0:T(2,128)(2,1)S(1)} all-gather(bf16[1,1,128]{2,1,0:T(2,128)(2,1)S(1)} %bitcast.59), channel_id=1, replica_groups=mesh['fsdp'=32] {'fsdp'}, dimensions={0}, use_global_device_ids=true | all-gather | bytes 8448 | tf_op jit(solution)/shard_map/all_gather | solution.py:94
  263.3 27.7 %multiply_convert_fusion.1 = (bf16[512,4096]{1,0:T(8,128)(2,1)}, f32[512,4096]{1,0:T(8,128)}, f32[512,4096]{1,0:T(8,128)}) fusion(f32[4096]{0:T(1024)S(1)} %bitcast.57, bf16[1024,4096]{1,0:T(8,128)(2,1)} %all-gather.10.cloned.1.call-done, bf16[512,1024]{1,0:T(8,128)(2,1)S(1)} %copy-done.1, f32[1024]{0:T(1024)S(1)} %convert_element_type.108, ...), kind=kOutput, calls=%fused_computation.10 | convolution fusion | flops 4436525056 | bytes 30437376 | tf_op jit(solution)/shard_map/dot_general | solution.py:141
  291.0 5.6 all-gather.12.cloned.1.call-done
  296.6 13.6 %convert_reduce_fusion = (f32[4096]{0:T(1024)S(1)}, bf16[512,4096]{1,0:T(8,128)(2,1)S(1)}) fusion(f32[512,4096]{1,0:T(8,128)} %get-tuple-element.78, bf16[4096,1024]{1,0:T(8,128)(2,1)} %all-gather.12.cloned.1.call-done, bf16[512,1024]{1,0:T(8,128)(2,1)S(1)} %copy-done.7, f32[512]{0:T(512)S(1)} %get-tuple-element.75, f32[512,4096]{1,0:T(8,128)} %get-tuple-element.103, ...), kind=kOutput, calls=%fused_computation.8 | convolution fusion | flops 4332187648 | bytes 30443520 | tf_op jit(solution)/shard_map/dot_general | solution.py:53
  310.2 2.1 copy-done.21
  312.3 8.6 fusion.51
  321.1 10.5 %fusion.59 = f32[4096,1024]{1,0:T(8,128)} fusion(bf16[512,4096]{1,0:T(8,128)(2,1)} %get-tuple-element.77, bf16[512,1024]{1,0:T(8,128)(2,1)S(1)} %copy-done.7, f32[512]{0:T(512)S(1)} %get-tuple-element.75), kind=kOutput, calls=%fused_computation.109 | convolution fusion | flops 4296540160 | bytes 22022144 | tf_op jit(solution)/shard_map/dot_general | solution.py:47
  331.7 0.6 copy-done.13
  333.2 2.0 convert_reduce_fusion.1
  335.2 6.8 fusion.58
  342.0 8.0 fusion.68
  350.0 2.2 convert_reduce_fusion.3
  352.3 44.7 %all-reduce.14 = (f32[3072]{0:T(1024)S(1)}, f32[1024]{0:T(1024)S(1)}, f32[4096]{0:T(1024)S(1)}, f32[1024]{0:T(1024)S(1)}, f32[1024]{0:T(1024)S(1)}, /*index=5*/f32[1024]{0:T(1024)S(1)}, f32[1024]{0:T(1024)S(1)}) all-reduce(f32[3072]{0:T(1024)S(1)} %convert_reduce_fusion.1, ...), channel_id=6, replica_groups=mesh['fsdp'=32] {'fsdp'}, use_global_device_ids=true, to_apply=%region_13.14.clone | all-reduce | flops 12288 | bytes 98304
  397.1 0.6 dynamic-slice.13
  399.4 0.6 dynamic-slice.10
  400.0 0.6 dynamic-slice.12
  400.6 8.3 fusion.75
  408.9 2.4 fusion.35
  411.3 186.0 %reduce-scatter.5.cloned.1.call-done = f32[32,3072]{1,0:T(8,128)} async-done(((f32[1024,3072]{1,0:T(8,128)}), f32[32,3072]{1,0:T(8,128)}) %reduce-scatter.5.cloned.1.call-update) | async-done | bytes 393232 | tf_op jit(solution)/shard_map/reduce_scatter | solution.py:218
  597.3 187.4 %reduce-scatter.9.cloned.1.call-done = f32[32,4096]{1,0:T(8,128)} async-done(((f32[1024,4096]{1,0:T(8,128)}), f32[32,4096]{1,0:T(8,128)}) %reduce-scatter.9.cloned.1.call-update) | async-done | bytes 524304 | tf_op jit(solution)/shard_map/reduce_scatter | solution.py:220
  784.7 187.5 %reduce-scatter.11.cloned.1.call-done = f32[128,1024]{1,0:T(8,128)} async-done(((f32[4096,1024]{1,0:T(8,128)}), f32[128,1024]{1,0:T(8,128)}) %reduce-scatter.11.cloned.1.call-update) | async-done | bytes 524304 | tf_op jit(solution)/shard_map/reduce_scatter | solution.py:221
  (94 shorter events, 6.2 us)
Async XLA Ops:
  7.2 131.7 %copy-start = (bf16[512,1024]{1,0:T(8,128)(2,1)S(1)}, bf16[512,1024]{1,0:T(8,128)(2,1)}, u32[]{:S(2)}) copy-start(bf16[512,1024]{1,0:T(8,128)(2,1)} %param.23) | copy-start | bytes 3145732
  7.2 59.7 %all-gather.8.cloned.1.call-start = ((), (), s32[]{:S(2)}) async-start(), calls=%async_computation.5 | async-start | bytes 2162688 | tf_op jit(solution)/shard_map/all_gather | solution.py:89
  7.9 131.0 %all-gather.6.cloned.1.call-start = ((), (), s32[]{:S(2)}) async-start(), calls=%async_computation.4 | async-start | bytes 6488064 | tf_op jit(solution)/shard_map/all_gather | solution.py:88
  8.7 254.6 %all-gather.10.cloned.1.call-start = ((), (), s32[]{:S(2)}) async-start(), calls=%async_computation.6 | async-start | bytes 8650752 | tf_op jit(solution)/shard_map/all_gather | solution.py:90
  9.4 287.2 %all-gather.12.cloned.1.call-start = ((), (), s32[]{:S(2)}) async-start(), calls=%async_computation.7 | async-start | bytes 8650752 | tf_op jit(solution)/shard_map/all_gather | solution.py:91
  10.0 401.3 %reduce-scatter.7.cloned.1.call-start = ((), (), s32[]{:S(2)}) async-start(), calls=%async_computation.9 | async-start | bytes 4325376 | tf_op jit(solution)/shard_map/reduce_scatter | solution.py:219
  57.4 81.5 %copy-start.10 = (f32[1024]{0:T(1024)}, f32[1024]{0:T(1024)S(1)}, u32[]{:S(2)}) copy-start(f32[1024]{0:T(1024)S(1)} %convert_element_type.97) | copy-start | bytes 12292
  152.9 15.2 %copy-start.4 = (bf16[512,16,48]{0,2,1:T(8,128)(2,1)}, bf16[512,16,48]{0,2,1:T(8,128)(2,1)S(1)}, u32[]{:S(2)}) copy-start(bf16[512,16,48]{0,2,1:T(8,128)(2,1)S(1)} %slice.142) | copy-start | bytes 2359300
  154.7 13.3 %copy-start.5 = (bf16[512,16,48]{0,2,1:T(8,128)(2,1)}, bf16[512,16,48]{0,2,1:T(8,128)(2,1)S(1)}, u32[]{:S(2)}) copy-start(bf16[512,16,48]{0,2,1:T(8,128)(2,1)S(1)} %slice.143) | copy-start | bytes 2359300
  157.4 10.7 %copy-start.9 = (bf16[512,1024]{0,1:T(8,128)(2,1)S(1)}, bf16[512,1024]{0,1:T(8,128)(2,1)}, u32[]{:S(2)}) copy-start(bf16[512,1024]{0,1:T(8,128)(2,1)} %copy.51) | copy-start | bytes 3145732
  168.0 8.5 copy-start.6
  175.5 1.0 copy-start.18
  179.9 417.4 %reduce-scatter.5.cloned.1.call-start = ((), (), s32[]{:S(2)}) async-start(), calls=%async_computation.8 | async-start | bytes 12976128 | tf_op jit(solution)/shard_map/reduce_scatter | solution.py:218
  180.2 14.4 %slice-start = ((s8[16777216]{0:T(1024)(128)(4,1)}), s8[4194304]{0:T(1024)(128)(4,1)S(1)}, s32[]{:S(2)}) async-start(s8[16777216]{0:T(1024)(128)(4,1)} %bitcast.38), calls=%async_computation.12 | async-start | bytes 8388608
  180.2 14.8 %slice-start.1 = ((s8[16777216]{0:T(1024)(128)(4,1)}), s8[4194304]{0:T(1024)(128)(4,1)S(1)}, s32[]{:S(2)}) async-start(s8[16777216]{0:T(1024)(128)(4,1)} %bitcast.38), calls=%async_computation.13 | async-start | bytes 8388608
  180.2 16.0 %slice-start.2 = ((s8[16777216]{0:T(1024)(128)(4,1)}), s8[4194304]{0:T(1024)(128)(4,1)S(1)}, s32[]{:S(2)}) async-start(s8[16777216]{0:T(1024)(128)(4,1)} %bitcast.38), calls=%async_computation.14 | async-start | bytes 8388608
  180.2 17.2 %slice-start.3 = ((s8[16777216]{0:T(1024)(128)(4,1)}), s8[4194304]{0:T(1024)(128)(4,1)S(1)}, s32[]{:S(2)}) async-start(s8[16777216]{0:T(1024)(128)(4,1)} %bitcast.38), calls=%async_computation.15 | async-start | bytes 8388608
  217.9 4.8 copy-start.11
  233.2 0.6 copy-start.15
  233.2 0.7 copy-start.14
  233.2 0.7 copy-start.16
  233.2 30.0 %copy-start.1 = (bf16[512,1024]{1,0:T(8,128)(2,1)S(1)}, bf16[512,1024]{1,0:T(8,128)(2,1)}, u32[]{:S(2)}) copy-start(bf16[512,1024]{1,0:T(8,128)(2,1)} %param.23) | copy-start | bytes 3145732
  233.3 551.5 %reduce-scatter.9.cloned.1.call-start = ((), (), s32[]{:S(2)}) async-start(), calls=%async_computation.10 | async-start | bytes 17301504 | tf_op jit(solution)/shard_map/reduce_scatter | solution.py:220
  263.3 33.4 %copy-start.7 = (bf16[512,1024]{1,0:T(8,128)(2,1)S(1)}, bf16[512,1024]{1,0:T(8,128)(2,1)}, u32[]{:S(2)}) copy-start(bf16[512,1024]{1,0:T(8,128)(2,1)} %param.25) | copy-start | bytes 3145732
  310.2 2.1 copy-start.21
  320.9 651.3 %reduce-scatter.11.cloned.1.call-start = ((), (), s32[]{:S(2)}) async-start(), calls=%async_computation.11 | async-start | bytes 17301504 | tf_op jit(solution)/shard_map/reduce_scatter | solution.py:221
  331.6 0.7 copy-start.13
  331.6 0.7 copy-start.12
  331.6 1.2 copy-start.2
  331.6 1.5 copy-start.3
  335.2 6.8 copy-start.22
  342.0 8.0 copy-start.8
  397.1 575.1 %copy-start.20 = (f32[32]{0:T(128)}, f32[32]{0:T(128)S(1)}, u32[]{:S(2)}) copy-start(f32[32]{0:T(128)S(1)} %dynamic-slice.11) | copy-start | bytes 388
  400.6 8.3 copy-start.17
  400.6 8.3 copy-start.19
Sparse Core Ops, SparseCore 0:
  10.9 55.9 all-gather.7
  69.8 69.1 all-gather.5
  141.8 75.9 all-gather.9
  220.5 76.0 all-gather.11
  299.3 108.0 reduce-scatter.6
  413.9 183.3 reduce-scatter.4
  600.3 184.4 reduce-scatter.8
  787.7 184.4 reduce-scatter.10
where the time goes:
time: 990 us; the launch traced here: 980 us
  waiting for transfers between devices  640 us (65%)
  matrix products  154 us (16%)
  blocking collectives  115 us (12%)
  local copies, waits for them, and re-layouts  32.4 us (3%)
  other arithmetic  23.2 us (2%)
  between operations  14.8 us (1%)
    reduce_scatter x1, waiting for transfers between devices, on_device(): lax.psum_scatter(grad_wdown, 'fsdp', scatter_dimension=0, tiled=True)  187 us
    reduce_scatter x1, waiting for transfers between devices, on_device(): lax.psum_scatter(grad_wup, 'fsdp', scatter_dimension=0, tiled=True)  187 us
    reduce_scatter x1, waiting for transfers between devices, on_device(): lax.psum_scatter(grad_wqkv, 'fsdp', scatter_dimension=0, tiled=True)  186 us
    unnamed x2, blocking collectives  86.2 us
    all_gather x1, waiting for transfers between devices, on_device(): lax.all_gather(w_qkv, 'fsdp', axis=0, tiled=True)  67.5 us
    dot_general x4, matrix products, inner_rows(): lax.dot_general(left_side, right_side, (((0,), (0,)), ((), ())), preferre...  32.9 us
    dot_general x4, matrix products, times_transpose(): lax.dot_general(left_side, right_side, (((1,), (1,)), ((), ())), preferre...  31.5 us
    all_gather x1, blocking collectives, on_device(): lax.all_gather(b_up, 'fsdp', axis=0, tiled=True)  29.3 us
  transfers between devices with their start and end apart: 8, of which 6 were waited for; matrix products, arithmetic and copies ran while one was open for 20% of the time, Pallas kernels for 0%

commit v1 on v0

--- a/solution.py
+++ b/solution.py
@@ -3,6 +3,8 @@
 import jax
 import jax.numpy as jnp
 from jax import lax
+from jax.experimental import pallas as pl
+from jax.experimental.pallas import tpu as pltpu
 from jax.sharding import PartitionSpec as P
 
 D = 1024
@@ -67,7 +69,7 @@
     return jnp.sum(values.astype(jnp.float32), axis=0)
 
 
-def on_device(
+def on_device_any(
     tokens,
     segment_ids,
     cotangent,
@@ -245,6 +247,538 @@
     )
 
 
+BF16 = jnp.bfloat16
+F32 = jnp.float32
+PLANE = 8
+LINE = 4
+DEVICES = PLANE * LINE
+SLOTS = 512
+HELD = PLANE * SLOTS
+FF_PART = 512
+QKV_PART = 384
+VMEM_BYTES = 56 * 1024 * 1024
+
+
+def exchange(values, partner):
+    return lax.ppermute(values, "fsdp", [(i, partner(i)) for i in range(DEVICES)])
+
+
+def swap_core(values):
+    return exchange(values, lambda i: i ^ 1)
+
+
+def swap_near(values):
+    return exchange(values, lambda i: i ^ (4 if i % 2 else 2))
+
+
+def swap_far(values):
+    return exchange(values, lambda i: i ^ (2 if i % 2 else 4))
+
+
+def over_groups(values, groups):
+    return lax.all_to_all(
+        values, "fsdp", split_axis=0, concat_axis=0, tiled=True, axis_index_groups=groups
+    )
+
+
+def over_plane(values):
+    return over_groups(values, [[PLANE * z + r for r in range(PLANE)] for z in range(LINE)])
+
+
+def over_line(values):
+    return over_groups(values, [[PLANE * z + r for z in range(LINE)] for r in range(PLANE)])
+
+
+def gather_line(values):
+    return over_line(jnp.broadcast_to(values[None], (LINE,) + values.shape))
+
+
+def sum_line(values):
+    return jnp.sum(over_line(values).astype(F32), axis=0)
+
+
+def spread_tokens(own):
+    pair = jnp.concatenate([own, swap_near(own)])
+    half = jnp.concatenate([pair, swap_far(pair)])
+    return jnp.concatenate([half, swap_core(half)])
+
+
+def add_low(left_side, right_side):
+    return (left_side.astype(F32) + right_side.astype(F32)).astype(BF16)
+
+
+def collect_tokens(part):
+    half = add_low(part[: HELD // 2], swap_core(part[HELD // 2 :]))
+    pair = add_low(half[: 2 * SLOTS], swap_far(half[2 * SLOTS :]))
+    return pair[:SLOTS].astype(F32) + swap_near(pair[SLOTS:]).astype(F32)
+
+
+def normalize(rows):
+    center = rows - jnp.mean(rows, axis=-1, keepdims=True)
+    inv_scale = lax.rsqrt(jnp.mean(center * center, axis=-1, keepdims=True) + epsilon)
+    return (center * inv_scale, inv_scale)
+
+
+def plain(left_side, right_side):
+    return lax.dot_general(
+        left_side, right_side, (((1,), (0,)), ((), ())), preferred_element_type=F32
+    )
+
+
+def swap_pairs(values):
+    lane = lax.broadcasted_iota(jnp.int32, values.shape, 1)
+    return jnp.where(
+        (lane & 8) == 0, pltpu.roll(values, 120, axis=1), pltpu.roll(values, 8, axis=1)
+    )
+
+
+def up_kernel(tok_ref, w_ref, gain_ref, shift_ref, bias_ref, h_ref, hidden_ref, slope_ref):
+    normed, _ = normalize(tok_ref[...].astype(F32))
+    h_low = (normed * gain_ref[...] + shift_ref[...]).astype(BF16)
+    h_ref[...] = h_low
+    pre = plain(h_low, w_ref[...]) + bias_ref[...]
+    cdf = 0.5 + 0.5 * lax.erf(pre * 0.5**0.5)
+    hidden_ref[...] = (pre * cdf).astype(BF16)
+    slope_ref[...] = cdf + pre * jnp.exp(-0.5 * pre * pre) * 0.3989422804014327
+
+
+def qkv_kernel(tok_ref, w_ref, gain_ref, shift_ref, bias_ref, cos_ref, sin_ref, h_ref, qkv_ref):
+    normed, _ = normalize(tok_ref[...].astype(F32))
+    h_low = (normed * gain_ref[...] + shift_ref[...]).astype(BF16)
+    h_ref[...] = h_low
+    joined = plain(h_low, w_ref[...]) + bias_ref[...]
+    cos_rows, sin_rows = cos_ref[...], sin_ref[...]
+    for part in range(2):
+        rows = joined[:, 128 * part : 128 * part + 128]
+        qkv_ref[:, 128 * part : 128 * part + 128] = (
+            rows * cos_rows + swap_pairs(rows) * sin_rows
+        ).astype(BF16)
+    qkv_ref[:, 256:] = joined[:, 256:].astype(BF16)
+
+
+def accumulate(total_ref, step, value):
+    @pl.when(step == 0)
+    def _():
+        total_ref[...] = value
+
+    @pl.when(step > 0)
+    def _():
+        total_ref[...] += value
+
+
+def down_kernel(
+    grad_ref, h_ref, hidden_ref, slope_ref, w_down_ref, w_up_ref, gain_ref,
+    branch_ref, dnorm_ref, dw_down_ref, dw_up_ref, db_ref, dot_ref, shift_ref,
+    down_acc, up_acc,
+):
+    step = pl.program_id(0)
+    grad, hidden = grad_ref[...], hidden_ref[...]
+    w_down, w_up = w_down_ref[...], w_up_ref[...]
+    d_pre = times_transpose(grad, w_down) * slope_ref[...]
+    d_low = d_pre.astype(BF16)
+    accumulate(db_ref, step, jnp.sum(d_low.astype(F32), axis=0, keepdims=True))
+    branch_ref[...] = plain(hidden, w_down).astype(BF16)
+    dnorm_ref[...] = (times_transpose(d_low, w_up) * gain_ref[...]).astype(BF16)
+    accumulate(down_acc, step, inner_rows(hidden, grad))
+    accumulate(up_acc, step, inner_rows(h_ref[...], d_low))
+
+    @pl.when(step == pl.num_programs(0) - 1)
+    def _():
+        dw_down_ref[...] = down_acc[...].astype(BF16)
+        dw_up_ref[...] = up_acc[...].astype(BF16)
+        weights = w_up.astype(F32)
+        dot_ref[...] = jnp.sum(weights * up_acc[...], axis=1, keepdims=True)
+        shift_ref[...] = jnp.sum(weights * db_ref[...], axis=1, keepdims=True)
+
+
+def attention_kernel(
+    grad_ref, qkv_ref, h_ref, cos_ref, sin_ref, seg_row_ref, seg_col_ref, w_out_ref, w_ref,
+    branch_ref, dmlp_ref, gain_ref,
+    out_ref, dnorm_ref, dw_out_ref, dw_ref, db_ref, dot_ref, shift_ref,
+    out_acc, acc,
+):
+    step = pl.program_id(0)
+    grad = grad_ref[...]
+    d_att = times_transpose(grad, w_out_ref[...]).astype(BF16)
+    seg_rows, seg_cols = seg_col_ref[...], seg_row_ref[0]
+    row_index = lax.broadcasted_iota(jnp.int32, (SLOTS, SLOTS), 0)
+    col_index = lax.broadcasted_iota(jnp.int32, (SLOTS, SLOTS), 1)
+    allowed = ((seg_rows == seg_cols) & (seg_cols >= 0) & (col_index <= row_index)) | (
+        col_index == row_index
+    )
+    attended, d_query, d_key, d_value = [], [], [], []
+    for head in range(2):
+        query = qkv_ref[:, 64 * head : 64 * head + 64]
+        key = qkv_ref[:, 128 + 64 * head : 192 + 64 * head]
+        value = qkv_ref[:, 256 + 64 * head : 320 + 64 * head]
+        d_head = d_att[:, 64 * head : 64 * head + 64]
+        scores = jnp.where(allowed, times_transpose(query, key) * HEAD_DIM ** (-0.5), -1e30)
+        weights = jnp.exp(scores - jnp.max(scores, axis=-1, keepdims=True))
+        prob = weights * (1.0 / jnp.sum(weights, axis=-1, keepdims=True))
+        prob_low = prob.astype(BF16)
+        attended.append(plain(prob_low, value))
+        d_prob = times_transpose(d_head, value)
+        row_dot = jnp.sum(prob * d_prob, axis=-1, keepdims=True)
+        d_score = (prob * (d_prob - row_dot)).astype(BF16)
+        d_query.append(plain(d_score, key) * HEAD_DIM ** (-0.5))
+        d_key.append(inner_rows(d_score, query) * HEAD_DIM ** (-0.5))
+        d_value.append(inner_rows(prob_low, d_head))
+    cos_rows, sin_rows = cos_ref[...], sin_ref[...]
+    turned = []
+    for parts in (d_query, d_key):
+        rows = jnp.concatenate(parts, axis=1)
+        turned.append(rows * cos_rows - swap_pairs(rows) * sin_rows)
+    att_low = jnp.concatenate(attended, axis=1).astype(BF16)
+    d_joined = jnp.concatenate(turned + d_value, axis=1).astype(BF16)
+    out_ref[...] = (plain(att_low, w_out_ref[...]) + branch_ref[...].astype(F32)).astype(BF16)
+    dnorm_ref[...] = (
+        times_transpose(d_joined, w_ref[...]) * gain_ref[...] + dmlp_ref[...].astype(F32)
+    ).astype(BF16)
+    accumulate(db_ref, step, jnp.sum(d_joined.astype(F32), axis=0, keepdims=True))
+    accumulate(out_acc, step, inner_rows(att_low, grad))
+    accumulate(acc, step, inner_rows(h_ref[...], d_joined))
+
+    @pl.when(step == pl.num_programs(0) - 1)
+    def _():
+        dw_out_ref[...] = out_acc[...].astype(BF16)
+        dw_ref[...] = acc[...].astype(BF16)
+        weights = w_ref[...].astype(F32)
+        dot_ref[...] = jnp.sum(weights * acc[...], axis=1, keepdims=True)
+        shift_ref[...] = jnp.sum(weights * db_ref[...], axis=1, keepdims=True)
+
+
+def tiled(width):
+    return pl.BlockSpec((SLOTS, width), lambda i: (i, 0))
+
+
+def kept(shape):
+    return pl.BlockSpec(shape, lambda i: (0,) * len(shape))
+
+
+def shaped(shape, dtype):
+    return jax.ShapeDtypeStruct(shape, dtype)
+
+
+def run(kernel, operands, in_specs, outs, out_specs, scratch, flops, moved, name):
+    return pl.pallas_call(
+        kernel,
+        grid=(PLANE,),
+        in_specs=in_specs,
+        out_specs=out_specs,
+        out_shape=outs,
+        scratch_shapes=scratch,
+        compiler_params=pltpu.CompilerParams(
+            vmem_limit_bytes=VMEM_BYTES, dimension_semantics=("arbitrary",)
+        ),
+        cost_estimate=pl.CostEstimate(flops=flops, bytes_accessed=moved, transcendentals=0),
+        name=name,
+    )(*operands)
+
+
+def run_up(held, w_up, gain, shift, bias):
+    return run(
+        up_kernel,
+        (held, w_up, gain, shift, bias),
+        [tiled(D), kept((D, FF_PART)), kept((1, D)), kept((1, D)), kept((1, FF_PART))],
+        [
+            shaped((HELD, D), BF16),
+            shaped((HELD, FF_PART), BF16),
+            shaped((HELD, FF_PART), F32),
+        ],
+        [tiled(D), tiled(FF_PART), tiled(FF_PART)],
+        [],
+        2 * HELD * D * FF_PART,
+        HELD * (4 * D + 6 * FF_PART),
+        "up",
+    )
+
+
+def run_qkv(held, w_qkv, gain, shift, bias, cos_rows, sin_rows):
+    return run(
+        qkv_kernel,
+        (held, w_qkv, gain, shift, bias, cos_rows, sin_rows),
+        [
+            tiled(D),
+            kept((D, QKV_PART)),
+            kept((1, D)),
+            kept((1, D)),
+            kept((1, QKV_PART)),
+            tiled(128),
+            tiled(128),
+        ],
+        [shaped((HELD, D), BF16), shaped((HELD, QKV_PART), BF16)],
+        [tiled(D), tiled(QKV_PART)],
+        [],
+        2 * HELD * D * QKV_PART,
+        HELD * (4 * D + 2 * QKV_PART + 1024),
+        "qkv",
+    )
+
+
+def run_down(grad, h_mlp, hidden, slope, w_down, w_up, gain):
+    return run(
+        down_kernel,
+        (grad, h_mlp, hidden, slope, w_down, w_up, gain),
+        [
+            tiled(D),
+            tiled(D),
+            tiled(FF_PART),
+            tiled(FF_PART),
+            kept((FF_PART, D)),
+            kept((D, FF_PART)),
+            kept((1, D)),
+        ],
+        [
+            shaped((HELD, D), BF16),
+            shaped((HELD, D), BF16),
+            shaped((FF_PART, D), BF16),
+            shaped((D, FF_PART), BF16),
+            shaped((1, FF_PART), F32),
+            shaped((D, 1), F32),
+            shaped((D, 1), F32),
+        ],
+        [
+            tiled(D),
+            tiled(D),
+            kept((FF_PART, D)),
+            kept((D, FF_PART)),
+            kept((1, FF_PART)),
+            kept((D, 1)),
+            kept((D, 1)),
+        ],
+        [pltpu.VMEM((FF_PART, D), F32), pltpu.VMEM((D, FF_PART), F32)],
+        10 * HELD * D * FF_PART,
+        HELD * (8 * D + 6 * FF_PART),
+        "down",
+    )
+
+
+def run_attention(
+    grad, qkv, h_attn, cos_rows, sin_rows, segments, w_out, w_qkv, branch, dmlp, gain
+):
+    return run(
+        attention_kernel,
+        (
+            grad, qkv, h_attn, cos_rows, sin_rows,
+            segments.reshape(PLANE, 1, SLOTS), segments.reshape(HELD, 1),
+            w_out, w_qkv, branch, dmlp, gain,
+        ),
+        [
+            tiled(D),
+            tiled(QKV_PART),
+            tiled(D),
+            tiled(128),
+            tiled(128),
+            pl.BlockSpec((1, 1, SLOTS), lambda i: (i, 0, 0)),
+            tiled(1),
+            kept((128, D)),
+            kept((D, QKV_PART)),
+            tiled(D),
+            tiled(D),
+            kept((1, D)),
+        ],
+        [
+            shaped((HELD, D), BF16),
+            shaped((HELD, D), BF16),
+            shaped((128, D), BF16),
+            shaped((D, QKV_PART), BF16),
+            shaped((1, QKV_PART), F32),
+            shaped((D, 1), F32),
+            shaped((D, 1), F32),
+        ],
+        [
+            tiled(D),
+            tiled(D),
+            kept((128, D)),
+            kept((D, QKV_PART)),
+            kept((1, QKV_PART)),
+            kept((D, 1)),
+            kept((D, 1)),
+        ],
+        [pltpu.VMEM((128, D), F32), pltpu.VMEM((D, QKV_PART), F32)],
+        4 * HELD * D * (QKV_PART + 128) + 24 * HELD * SLOTS * 256,
+        HELD * 12 * D,
+        "attention",
+    )
+
+
+def rotary_rows(segments):
+    index = jnp.arange(SLOTS, dtype=jnp.int32)[None, :]
+    start = jnp.zeros_like(segments)
+    for number in range(-1, 4):
+        first = jnp.min(jnp.where(segments == number, index, SLOTS), axis=1, keepdims=True)
+        start = jnp.where(segments == number, first, start)
+    position = (index - start).astype(F32).reshape(HELD, 1)
+    lane = jnp.arange(128, dtype=jnp.int32) % HEAD_DIM
+    inv_freq = 10000.0 ** (-(lane % 8).astype(F32) * 2.0 / ROTARY)
+    angles = position * jnp.where(lane < ROTARY, inv_freq, 0.0)[None, :]
+    sign = jnp.where(lane < ROTARY // 2, -1.0, 1.0)
+    return (jnp.cos(angles), jnp.sin(angles) * sign[None, :])
+
+
+def on_device_plane(
+    tokens, segment_ids, cotangent, w_qkv, w_out, w_up, w_down,
+    b_qkv, b_out, b_up, b_down, gain_attn, shift_attn, gain_mlp, shift_mlp,
+):
+    me = lax.axis_index("fsdp")
+    rank, core, chip = me % PLANE, me % 2, (me % PLANE) // 2
+    rows = w_up.shape[0]
+
+    up_cuts = w_up.reshape(rows, LINE, PLANE, 128).transpose(2, 0, 1, 3)
+    qkv_cuts = w_qkv.reshape(rows, 3, 2, 2, 4, HEAD_DIM).transpose(4, 2, 0, 1, 3, 5)
+    vectors = jnp.concatenate(
+        [b_qkv, b_out, b_up, b_down, gain_attn, shift_attn, gain_mlp, shift_mlp]
+    )
+    block = jnp.concatenate(
+        [
+            jnp.pad(vectors, (0, 512 - vectors.shape[0])).reshape(4, 128),
+            segment_ids.astype(BF16).reshape(4, 128),
+            jnp.zeros((rows - 8, 128), BF16),
+        ]
+    )
+    got = over_plane(
+        jnp.concatenate(
+            [
+                up_cuts.reshape(PLANE, rows, FF_PART),
+                jnp.broadcast_to(block[None], (PLANE, rows, 128)),
+                qkv_cuts.reshape(PLANE, rows, QKV_PART),
+            ],
+            axis=2,
+        )
+    ).reshape(PLANE * rows, 1024)
+    up_all = gather_line(got[:, :640]).reshape(D, 640)
+    down_all = gather_line(jnp.concatenate([w_down, w_out]))
+    qkv_part = gather_line(got[:, 640:]).reshape(D, QKV_PART)
+    up_part = up_all[:, :FF_PART]
+    down_part = down_all[:, :128].reshape(FF_PART, D)
+
+    held = spread_tokens(tokens)
+    live_rows = (segment_ids >= 0).astype(F32)
+    grad_out = cotangent.astype(F32) * live_rows[:, None]
+    grad_own = grad_out.astype(BF16)
+    grad = spread_tokens(grad_own)
+
+    halves = down_all[:, 128:]
+    mine = lax.dynamic_slice_in_dim(halves, 2 * core, 2)
+    theirs = swap_core(lax.dynamic_slice_in_dim(halves, 2 - 2 * core, 2))
+    out_part = jnp.where(
+        core == 0, jnp.stack([mine, theirs], axis=1), jnp.stack([theirs, mine], axis=1)
+    ).reshape(128, D)
+
+    vec = up_all[:, FF_PART:].reshape(DEVICES, rows, 128)[:, :4].reshape(DEVICES, 512)
+    vec = vec.astype(F32)
+    qkv_bias = vec[:, :96].reshape(3, 2, 2, 4, HEAD_DIM)
+    qkv_bias = lax.dynamic_index_in_dim(qkv_bias, chip, 3, keepdims=False)
+    qkv_bias = lax.dynamic_index_in_dim(qkv_bias, core, 1, keepdims=False).reshape(1, QKV_PART)
+    up_bias = vec[:, 128:256].reshape(LINE, PLANE, 128)
+    up_bias = lax.dynamic_index_in_dim(up_bias, rank, 1, keepdims=False).reshape(1, FF_PART)
+    out_bias = (vec[:, 96:128] + vec[:, 256:288]).reshape(1, D)
+    gain_one, shift_one, gain_two, shift_two = (
+        vec[:, 288 + 32 * i : 320 + 32 * i].reshape(1, D) for i in range(4)
+    )
+
+    near = 2 + 2 * core
+    far = 6 - near
+    order = jnp.stack(
+        [
+            rank, rank ^ near, rank ^ far, rank ^ 6,
+            rank ^ 1, rank ^ 1 ^ far, rank ^ 1 ^ near, rank ^ 7,
+        ]
+    )
+    seg_all = got[:, FF_PART:640].reshape(PLANE, rows, 128)[:, 4:8].reshape(PLANE, SLOTS)
+    segments = jnp.take(seg_all, order, axis=0).astype(jnp.int32)
+    cos_rows, sin_rows = rotary_rows(segments)
+
+    h_mlp, hidden, slope = run_up(held, up_part, gain_two, shift_two, up_bias)
+    h_attn, qkv = run_qkv(held, qkv_part, gain_one, shift_one, qkv_bias, cos_rows, sin_rows)
+    branch, dmlp, dw_down, dw_up, db_up, dot_two, sum_two = run_down(
+        grad, h_mlp, hidden, slope, down_part, up_part, gain_two
+    )
+    out_sum, dnorm_sum, dw_out, dw_qkv, db_qkv, dot_one, sum_one = run_attention(
+        grad, qkv, h_attn, cos_rows, sin_rows, segments, out_part, qkv_part, branch, dmlp, gain_one
+    )
+
+    grad_w_down = sum_line(dw_down.reshape(LINE, 128, D))
+    up_rows = sum_line(dw_up.reshape(LINE, PLANE * rows, FF_PART)).astype(BF16)
+    up_rows = over_plane(up_rows.reshape(PLANE, rows, FF_PART))
+    grad_w_up = (
+        up_rows.reshape(PLANE, rows, LINE, 128).transpose(1, 2, 0, 3).reshape(rows, 4 * D)
+    ).astype(F32)
+
+    pieces = dw_out.reshape(2, 2, 32, D)
+    mine = lax.dynamic_index_in_dim(pieces, core, 1, keepdims=False)
+    theirs = swap_core(lax.dynamic_index_in_dim(pieces, 1 - core, 1, keepdims=False))
+    pieces = jnp.where(
+        core == 0, jnp.concatenate([mine, theirs]), jnp.concatenate([theirs, mine])
+    )
+    pieces = pieces.reshape(LINE, 32, 8, 128).transpose(0, 2, 1, 3).reshape(LINE, 256, 128)
+    last = sum_line(
+        jnp.concatenate([dw_qkv.reshape(LINE, PLANE * rows, QKV_PART), pieces], axis=2)
+    )
+    grad_w_out = last[:, QKV_PART:].reshape(8, 32, 128).transpose(1, 0, 2).reshape(32, D)
+    qkv_rows = over_plane(last[:, :QKV_PART].astype(BF16).reshape(PLANE, rows, QKV_PART))
+    grad_w_qkv = (
+        qkv_rows.reshape(4, 2, rows, 3, 2, HEAD_DIM)
+        .transpose(2, 3, 1, 4, 0, 5)
+        .reshape(rows, 3 * D)
+        .astype(F32)
+    )
+
+    def at(index, count):
+        return (jnp.arange(count) == index).astype(F32)
+
+    db_qkv = db_qkv.reshape(3, 1, 2, 1, HEAD_DIM)
+    db_qkv = db_qkv * at(core, 2)[:, None, None, None] * at(chip, 4)[:, None]
+    db_up = db_up.reshape(LINE, 1, 128) * at(rank, PLANE)[:, None]
+    dot_one, sum_one = dot_one.reshape(1, D), sum_one.reshape(1, D)
+    dot_two, sum_two = dot_two.reshape(1, D), sum_two.reshape(1, D)
+    sums = jnp.concatenate(
+        [
+            db_qkv.reshape(DEVICES, 96),
+            column_sums(grad_own).reshape(DEVICES, 32),
+            db_up.reshape(DEVICES, 128),
+            ((dot_one - shift_one * sum_one) / gain_one).reshape(DEVICES, 32),
+            sum_one.reshape(DEVICES, 32),
+            ((dot_two - shift_two * sum_two) / gain_two).reshape(DEVICES, 32),
+            sum_two.reshape(DEVICES, 32),
+        ],
+        axis=1,
+    )
+    sums = over_groups(sums.reshape(DEVICES, 3, 128), None)
+    sums = jnp.sum(sums, axis=0).reshape(384)
+
+    inputs = tokens.astype(F32)
+    layer_out = (inputs + collect_tokens(out_sum) + out_bias).astype(BF16)
+    normed, inv_scale = normalize(inputs)
+    d_norm = collect_tokens(dnorm_sum)
+    d_inner = (
+        d_norm
+        - jnp.mean(d_norm, axis=-1, keepdims=True)
+        - normed * jnp.mean(d_norm * normed, axis=-1, keepdims=True)
+    )
+    tokens_grad = grad_out + d_inner * inv_scale
+    return (
+        layer_out,
+        tokens_grad,
+        grad_w_qkv,
+        grad_w_out,
+        grad_w_up,
+        grad_w_down,
+        sums[:96],
+        sums[96:128],
+        sums[128:256],
+        sums[96:128],
+        sums[256:288],
+        sums[288:320],
+        sums[320:352],
+        sums[352:384],
+    )
+
+
+def choose(mesh):
+    return on_device_plane if mesh.shape["fsdp"] == DEVICES else on_device_any
+
+
 def solution(mesh):
     in_specs = (
         P("fsdp", None),
@@ -280,5 +814,5 @@
         P("fsdp"),
     )
     return jax.shard_map(
-        on_device, mesh=mesh, in_specs=in_specs, out_specs=out_specs, check_vma=False
-    )
+        choose(mesh), mesh=mesh, in_specs=in_specs, out_specs=out_specs, check_vma=False
+    )

time: 990 us -> 460 us (0.46)
  waiting for transfers between devices: 640 us -> 122 us
  matrix products: 154 us -> 0 us
  Pallas kernels: 0 us -> 115 us
  blocking collectives: 115 us -> 10.3 us
  starting transfers between devices: 0.7 us -> 65.2 us
  other arithmetic: 23.2 us -> 67 us
  local copies, waits for them, and re-layouts: 32.4 us -> 74.1 us
  between operations: 14.8 us -> 1.18 us
    reduce_scatter x4 -> x0, waiting for transfers between devices: 561 us -> none  [the longest x1 187 us: on_device(): lax.psum_scatter(grad_wdown, 'fsdp', scatter_dimension=0, tiled=True)]
    dot_general x17 -> x0, matrix products: 143 us -> none  [the longest x4 32.9 us: inner_rows(): lax.dot_general(left_side, right_side, (((0,), (0,)), ((), ())), preferre...]
    pallas_call x0 -> x4, Pallas kernels: none -> 115 us  [run(): pl.pallas_call(kernel, grid=(PLANE,), in_specs=in_specs, out_specs=out_sp...]
    all_to_all x0 -> x9, waiting for transfers between devices: none -> 90.1 us  [over_groups(): lax.all_to_all(values, 'fsdp', split_axis=0, concat_axis=0, tiled=True, a...]
    unnamed x2 -> x0, blocking collectives: 86.2 us -> none
    all_gather x4 -> x0, waiting for transfers between devices: 76 us -> none  [the longest x1 67.5 us: on_device(): lax.all_gather(w_qkv, 'fsdp', axis=0, tiled=True)]
    all_to_all x0 -> x9, starting transfers between devices: none -> 56.4 us  [over_groups(): lax.all_to_all(values, 'fsdp', split_axis=0, concat_axis=0, tiled=True, a...]
    ppermute x0 -> x14, waiting for transfers between devices: none -> 31.9 us  [exchange(): lax.ppermute(values, 'fsdp', [(i, partner(i)) for i in range(DEVICES)])]
  transfers between devices with their start and end apart: 8 -> 23, of which waited for: 6 -> 12; matrix products, arithmetic and copies ran while one was open for 20% -> 28% of each run, Pallas kernels for 0% -> 12%
where the time goes in v1:
time: 460 us; the launch traced here: 455 us
  waiting for transfers between devices  122 us (27%)
  Pallas kernels  115 us (25%)
  local copies, waits for them, and re-layouts  74.1 us (16%)
  other arithmetic  67 us (15%)
  starting transfers between devices  65.2 us (14%)
  blocking collectives  10.3 us (2%)
    pallas_call x4, Pallas kernels, run(): pl.pallas_call(kernel, grid=(PLANE,), in_specs=in_specs, out_specs=out_sp...  115 us
    all_to_all x9, waiting for transfers between devices, over_groups(): lax.all_to_all(values, 'fsdp', split_axis=0, concat_axis=0, tiled=True, a...  90.1 us
    all_to_all x9, starting transfers between devices, over_groups(): lax.all_to_all(values, 'fsdp', split_axis=0, concat_axis=0, tiled=True, a...  56.4 us
    ppermute x14, waiting for transfers between devices, exchange(): lax.ppermute(values, 'fsdp', [(i, partner(i)) for i in range(DEVICES)])  31.9 us
    convert_element_type x4, other arithmetic, add_low(): return (left_side.astype(F32) + right_side.astype(F32)).astype(BF16)  17.5 us
    unnamed x68, local copies, waits for them, and re-layouts  15.3 us
    all_to_all x1, blocking collectives, over_groups(): lax.all_to_all(values, 'fsdp', split_axis=0, concat_axis=0, tiled=True, a...  10.3 us
    mul x1, other arithmetic, rotary_rows(): return (jnp.cos(angles), jnp.sin(angles) * sign[None, :])  9.34 us
  transfers between devices with their start and end apart: 23, of which 12 were waited for; matrix products, arithmetic and copies ran while one was open for 28% of the time, Pallas kernels for 12%

profile of v1, /device:TPU:14, one launch (start us, length us, event | category | flops | bytes accessed | tf_op | source)
XLA Modules:
  0.0 455.2 jit_solution(9565882480580508348)
XLA Ops:
  1.9 1.6 convert_reduce_fusion.1
  3.5 1.6 collective-permute-start
  5.1 10.6 %collective-permute-done.3 = bf16[512,1024]{1,0:T(8,128)(2,1)S(1)} collective-permute-done((bf16[512,1024]{1,0:T(8,128)(2,1)}, bf16[512,1024]{1,0:T(8,128)(2,1)S(1)}, u32[]{:S(2)}, u32[]{:S(2)}) %collective-permute-start.3) | collective-permute-done | bytes 1048608 | tf_op jit(solution)/shard_map/ppermute | solution.py:263
  15.7 3.1 pad_maximum_fusion.4
  24.0 4.8 %concatenate.79 = bf16[416]{0:T(512)(128)(2,1)S(1)} concatenate(bf16[96]{0:T(256)(128)(2,1)S(1)} %copy-done.25, bf16[32]{0:T(256)(128)(2,1)} %param.23, bf16[128]{0:T(256)(128)(2,1)} %param.24, bf16[32]{0:T(256)(128)(2,1)} %param.25, bf16[32]{0:T(256)(128)(2,1)} %param.26, bf16[32]{0:T(256)(128)(2,1)} %param.27, bf16[32]{0:T(256)(128)(2,1)} %param.28, bf16[32]{0:T(256)(128)(2,1)} %param.29), dimensions={0} | concatenate | bytes 1664 | tf_op jit(solution)/shard_map/concatenate | solution.py:629
  28.8 4.5 collective-permute-done
  33.2 1.5 pad_maximum_fusion.3
  36.2 5.7 %all-to-all-start = ((bf16[8,32,1024]{2,1,0:T(8,128)(2,1)}), bf16[8,32,1024]{2,1,0:T(8,128)(2,1)}, u32[]{:S(2)}, u32[]{:S(2)}) async-start(bf16[8,32,1024]{2,1,0:T(8,128)(2,1)} %pad_maximum_fusion.6), calls=%async_computation | async-start | bytes 1048576 | tf_op jit(solution)/shard_map/all_to_all | solution.py:279
  42.8 34.8 %all-to-all-done = bf16[8,32,1024]{2,1,0:T(8,128)(2,1)} async-done(((bf16[8,32,1024]{2,1,0:T(8,128)(2,1)}), bf16[8,32,1024]{2,1,0:T(8,128)(2,1)}, u32[]{:S(2)}, u32[]{:S(2)}) %all-to-all-start) | async-done | bytes 524320 | tf_op jit(solution)/shard_map/all_to_all | solution.py:279
  78.8 5.3 %all-to-all-start.3 = ((bf16[4,160,1024]{2,1,0:T(8,128)(2,1)}), bf16[4,160,1024]{2,1,0:T(8,128)(2,1)}, u32[]{:S(2)}, u32[]{:S(2)}) async-start(bf16[4,160,1024]{2,1,0:T(8,128)(2,1)} %broadcast_in_dim.149), calls=%async_computation.3 | async-start | bytes 2621440 | tf_op jit(solution)/shard_map/all_to_all | solution.py:279
  85.4 3.6 pad_maximum_fusion.2
  89.0 3.5 pad_maximum_fusion.1
  94.9 1.6 slice.160
  97.4 13.7 %all-to-all-done.3 = bf16[4,160,1024]{2,1,0:T(8,128)(2,1)} async-done(((bf16[4,160,1024]{2,1,0:T(8,128)(2,1)}), bf16[4,160,1024]{2,1,0:T(8,128)(2,1)}, u32[]{:S(2)}, u32[]{:S(2)}) %all-to-all-start.3) | async-done | bytes 1310752 | tf_op jit(solution)/shard_map/all_to_all | solution.py:279
  112.3 7.6 %all-to-all-start.2 = ((bf16[4,256,640]{2,1,0:T(8,128)(2,1)}), bf16[4,256,640]{2,1,0:T(8,128)(2,1)}, u32[]{:S(2)}, u32[]{:S(2)}) async-start(bf16[4,256,640]{2,1,0:T(8,128)(2,1)} %broadcast_in_dim.131), calls=%async_computation.2 | async-start | bytes 2621440 | tf_op jit(solution)/shard_map/all_to_all | solution.py:279
  120.2 2.0 copy.58
  122.8 9.3 %fusion.9 = (f32[4096,128]{1,0:T(8,128)}, f32[4096,128]{1,0:T(8,128)}) fusion(f32[128]{0:T(128)S(1)} %get-tuple-element.81, f32[128]{0:T(128)S(1)} %get-tuple-element.82, f32[4096]{0:T(1024)S(1)} %bitcast.142), kind=kLoop, calls=%fused_computation.22 | loop fusion | flops 1048576 | bytes 4211712 | tf_op jit(solution)/shard_map/mul | solution.py:616
  134.4 2.3 slice.174
  137.4 10.2 %all-to-all-done.2 = bf16[4,256,640]{2,1,0:T(8,128)(2,1)} async-done(((bf16[4,256,640]{2,1,0:T(8,128)(2,1)}), bf16[4,256,640]{2,1,0:T(8,128)(2,1)}, u32[]{:S(2)}, u32[]{:S(2)}) %all-to-all-start.2) | async-done | bytes 1310752 | tf_op jit(solution)/shard_map/all_to_all | solution.py:279
  148.5 7.5 %all-to-all-start.1 = ((bf16[4,256,384]{2,1,0:T(8,128)(2,1)}), bf16[4,256,384]{2,1,0:T(8,128)(2,1)}, u32[]{:S(2)}, u32[]{:S(2)}) async-start(bf16[4,256,384]{2,1,0:T(8,128)(2,1)} %broadcast_in_dim.130), calls=%async_computation.1 | async-start | bytes 1572864 | tf_op jit(solution)/shard_map/all_to_all | solution.py:279
  157.0 2.3 slice.170.w_ref.w_up_ref
  163.4 3.2 constant_dynamic-update-slice_fusion.1
  166.6 4.6 %constant_dynamic-update-slice_fusion.tok_ref = bf16[4096,1024]{1,0:T(8,128)(2,1)} fusion(bf16[4096,1024]{1,0:T(8,128)(2,1)} %constant_dynamic-update-slice_fusion.1, bf16[2048,1024]{1,0:T(8,128)(2,1)} %collective-permute-done.5), kind=kLoop, calls=%fused_computation.71 | loop fusion | bytes 8388608 | tf_op jit(solution)/shard_map/concatenate | solution.py:303
  171.2 15.8 %up.1 = (bf16[4096,1024]{1,0:T(8,128)(2,1)}, bf16[4096,512]{1,0:T(8,128)(2,1)}, f32[4096,512]{1,0:T(8,128)}) custom-call(bf16[4096,1024]{1,0:T(8,128)(2,1)} %constant_dynamic-update-slice_fusion.tok_ref, bf16[1024,512]{1,0:T(8,128)(2,1)} %slice.170.w_ref.w_up_ref, f32[1,1024]{1,0:T(1,128)} %reshape.784.gain_ref, f32[1,1024]{1,0:T(1,128)} %reshape.785.shift_ref, ...), custom_call_target="tpu_custom_call" | custom-call | flops 4294967296 | bytes 29360128 | tf_op jit(solution)/shard_map/up/pallas_call | solution.py:463
  186.9 6.6 %pad_maximum_fusion.grad_ref = bf16[4096,1024]{1,0:T(8,128)(2,1)} fusion(bf16[2048,1024]{1,0:T(8,128)(2,1)} %collective-permute-done.2, bf16[1024,1024]{1,0:T(8,128)(2,1)} %collective-permute-done.1, bf16[512,1024]{1,0:T(8,128)(2,1)S(1)} %collective-permute-done, bf16[512,1024]{1,0:T(8,128)(2,1)S(1)} %get-tuple-element.60), kind=kLoop, calls=%fused_computation.1 | loop fusion | flops 33554432 | bytes 16777216 | tf_op jit(solution)/shard_map/concatenate | solution.py:303
  193.6 36.7 %down.1 = (bf16[4096,1024]{1,0:T(8,128)(2,1)}, bf16[4096,1024]{1,0:T(8,128)(2,1)}, bf16[512,1024]{1,0:T(8,128)(2,1)}, bf16[1024,512]{1,0:T(8,128)(2,1)}, f32[1,5...) custom-call(bf16[4096,1024]{1,0:T(8,128)(2,1)} %pad_maximum_fusion.grad_ref, ...), custom_call_target="tpu_custom_call" | custom-call | flops 21474836480 | bytes 46137344 | tf_op jit(solution)/shard_map/down/pallas_call | solution.py:463
  230.3 14.0 %qkv.1 = (bf16[4096,1024]{1,0:T(8,128)(2,1)}, bf16[4096,384]{1,0:T(8,128)(2,1)}) custom-call(bf16[4096,1024]{1,0:T(8,128)(2,1)} %constant_dynamic-update-slice_fusion.tok_ref, bf16[1024,384]{1,0:T(8,128)(2,1)} %bitcast.5.w_ref, f32[1,1024]{1,0:T(1,128)} %reshape.778.gain_ref, f32[1,1024]{1,0:T(1,128)} %reshape.779.shift_ref, f32[1,384]{1,0:T(1,128)} %reshape.781.bias_ref, ...), custom_call_target="tpu_custom_call" | custom-call | flops 3221225472 | bytes 24117248 | tf_op jit(solution)/shard_map/qkv/pallas_call | solution.py:463
  244.3 48.9 %attention.1 = (bf16[4096,1024]{1,0:T(8,128)(2,1)}, bf16[4096,1024]{1,0:T(8,128)(2,1)}, bf16[128,1024]{1,0:T(8,128)(2,1)}, bf16[1024,384]{1,0:T(8,128)(2,1)}, f3...) custom-call(bf16[4096,1024]{1,0:T(8,128)(2,1)} %pad_maximum_fusion.grad_ref, ...), custom_call_target="tpu_custom_call" | custom-call | flops 21474836480 | bytes 50331648 | tf_op jit(solution)/shard_map/attention/pallas_call | solution.py:463
  293.3 4.9 %slice.143 = bf16[2048,1024]{1,0:T(8,128)(2,1)} slice(bf16[4096,1024]{1,0:T(8,128)(2,1)} %get-tuple-element.41), slice={[2048:4096], [0:1024]} | slice | bytes 8388608 | tf_op jit(solution)/shard_map/slice | solution.py:311
  299.4 2.4 slice.135
  303.9 10.3 %all_to_all.50 = f32[32,3,128]{2,1,0:T(4,128)S(1)} all-to-all(f32[32,3,128]{2,1,0:T(4,128)S(1)} %reshape.803), channel_id=1, replica_groups=mesh['fsdp'=32] {'fsdp'}, dimensions={0} | all-to-all | bytes 98304 | tf_op jit(solution)/shard_map/all_to_all | solution.py:279
  314.2 4.9 %all-to-all-start.6 = ((bf16[4,256,512]{2,1,0:T(8,128)(2,1)}), bf16[4,256,512]{2,1,0:T(8,128)(2,1)S(1)}, u32[]{:S(2)}, u32[]{:S(2)}) async-start(bf16[4,256,512]{2,1,0:T(8,128)(2,1)} %bitcast.42), calls=%async_computation.6 | async-start | bytes 2097152 | tf_op jit(solution)/shard_map/all_to_all | solution.py:279
  319.2 1.3 collective-permute-done.13
  320.6 2.2 pad_maximum_fusion.5
  322.8 19.1 %all-to-all-done.6 = bf16[4,256,512]{2,1,0:T(8,128)(2,1)S(1)} async-done(((bf16[4,256,512]{2,1,0:T(8,128)(2,1)}), bf16[4,256,512]{2,1,0:T(8,128)(2,1)S(1)}, u32[]{:S(2)}, u32[]{:S(2)}) %all-to-all-start.6) | async-done | bytes 1048608 | tf_op jit(solution)/shard_map/all_to_all | solution.py:279
  341.9 6.8 %all-to-all-start.4 = ((bf16[4,256,512]{2,1,0:T(8,128)(2,1)}), bf16[4,256,512]{2,1,0:T(8,128)(2,1)S(1)}, u32[]{:S(2)}, u32[]{:S(2)}) async-start(bf16[4,256,512]{2,1,0:T(8,128)(2,1)} %pad_maximum_fusion.5), calls=%async_computation.4 | async-start | bytes 2097152 | tf_op jit(solution)/shard_map/all_to_all | solution.py:279
  348.7 5.6 %add_convert_fusion = bf16[2048,1024]{1,0:T(8,128)(2,1)S(1)} fusion(bf16[2048,1024]{1,0:T(8,128)(2,1)} %collective-permute-done.10, bf16[4096,1024]{1,0:T(8,128)(2,1)} %get-tuple-element.41), kind=kLoop, calls=%fused_computation.2 | loop fusion | flops 8388608 | bytes 12582912 | tf_op jit(solution)/shard_map/convert_element_type | solution.py:307
  354.3 1.7 slice.182
  356.0 1.3 collective-permute-start.11
  357.3 5.6 %add_convert_fusion.1 = bf16[2048,1024]{1,0:T(8,128)(2,1)S(1)} fusion(bf16[2048,1024]{1,0:T(8,128)(2,1)} %collective-permute-done.7, bf16[4096,1024]{1,0:T(8,128)(2,1)} %get-tuple-element.40), kind=kLoop, calls=%fused_computation.3 | loop fusion | flops 8388608 | bytes 12582912 | tf_op jit(solution)/shard_map/convert_element_type | solution.py:307
  362.9 1.9 copy-done.1
  364.8 1.5 slice.176
  367.3 3.5 all-to-all-done.4
  370.8 7.5 %all-to-all-start.8 = ((bf16[4,128,1024]{2,1,0:T(8,128)(2,1)}), bf16[4,128,1024]{2,1,0:T(8,128)(2,1)}, u32[]{:S(2)}, u32[]{:S(2)}) async-start(bf16[4,128,1024]{2,1,0:T(8,128)(2,1)} %bitcast.45), calls=%async_computation.8 | async-start | bytes 2097152 | tf_op jit(solution)/shard_map/all_to_all | solution.py:279
  379.0 3.3 collective-permute-done.11
  382.3 3.2 add_convert_fusion.2
  386.6 1.4 collective-permute-start.12
  388.6 2.2 reduce_sum.89
  390.7 1.4 convert_reduce_fusion.3
  393.6 6.5 %all-to-all-done.8 = bf16[4,128,1024]{2,1,0:T(8,128)(2,1)} async-done(((bf16[4,128,1024]{2,1,0:T(8,128)(2,1)}), bf16[4,128,1024]{2,1,0:T(8,128)(2,1)}, u32[]{:S(2)}, u32[]{:S(2)}) %all-to-all-start.8) | async-done | bytes 1048608 | tf_op jit(solution)/shard_map/all_to_all | solution.py:279
  400.2 5.8 %all-to-all-start.7 = ((bf16[8,32,512]{2,1,0:T(8,128)(2,1)}), bf16[8,32,512]{2,1,0:T(8,128)(2,1)S(1)}, u32[]{:S(2)}, u32[]{:S(2)}) async-start(bf16[8,32,512]{2,1,0:T(8,128)(2,1)} %bitcast.116), calls=%async_computation.7 | async-start | bytes 524288 | tf_op jit(solution)/shard_map/all_to_all | solution.py:279
  406.0 12.2 %collective-permute-done.8 = bf16[1024,1024]{1,0:T(8,128)(2,1)} collective-permute-done((bf16[1024,1024]{1,0:T(8,128)(2,1)}, bf16[1024,1024]{1,0:T(8,128)(2,1)}, u32[]{:S(2)}, u32[]{:S(2)}) %collective-permute-start.8) | collective-permute-done | bytes 2097184 | tf_op jit(solution)/shard_map/ppermute | solution.py:263
  418.2 3.2 add_convert_fusion.3
  421.4 1.3 copy-done.6
  423.7 1.4 collective-permute-start.9
  425.1 5.3 %all-to-all-start.5 = ((bf16[8,32,384]{2,1,0:T(8,128)(2,1)}), bf16[8,32,384]{2,1,0:T(8,128)(2,1)}, u32[]{:S(2)}, u32[]{:S(2)}) async-start(bf16[8,32,384]{2,1,0:T(8,128)(2,1)} %bitcast.125), calls=%async_computation.5 | async-start | bytes 393216 | tf_op jit(solution)/shard_map/all_to_all | solution.py:279
  432.8 2.3 convert_reduce_fusion.2
  436.7 1.3 copy.48
  439.1 2.3 all-to-all-done.5
  441.4 2.3 reshape.812
  443.7 2.5 copy.46
  446.3 2.5 reshape.808
  448.8 2.2 fusion.13
  451.0 3.7 fusion.7
  (175 shorter events, 40.5 us)
Async XLA Ops:
  0.6 15.1 %collective-permute-start.3 = (bf16[512,1024]{1,0:T(8,128)(2,1)}, bf16[512,1024]{1,0:T(8,128)(2,1)S(1)}, u32[]{:S(2)}, u32[]{:S(2)}) collective-permute-start(bf16[512,1024]{1,0:T(8,128)(2,1)} %param.15), channel_id=1, source_target_pairs={{0,2},{1,5},{2,0},{3,7},{4,6},{5,1},{6,4},{7,3},{8,10},{9,13},{10,... | collective-permute-start | bytes 3145736 | tf_op jit(solution)/shard_map/ppermute | solution.py:263
  1.9 17.4 %copy-start.19 = (bf16[32,3072]{1,0:T(8,128)(2,1)S(1)}, bf16[32,3072]{1,0:T(8,128)(2,1)}, u32[]{:S(2)}) copy-start(bf16[32,3072]{1,0:T(8,128)(2,1)} %param.18) | copy-start | bytes 589828
  3.5 20.5 %copy-start.25 = (bf16[96]{0:T(256)(128)(2,1)S(1)}, bf16[96]{0:T(256)(128)(2,1)}, u32[]{:S(2)}) copy-start(bf16[96]{0:T(256)(128)(2,1)} %param.22) | copy-start | bytes 580
  3.5 25.2 %copy-start.22 = (s32[512]{0:T(512)S(1)}, s32[512]{0:T(512)}, u32[]{:S(2)}) copy-start(s32[512]{0:T(512)} %param.16) | copy-start | bytes 6148
  3.5 29.7 %collective-permute-start = (bf16[512,1024]{1,0:T(8,128)(2,1)S(1)}, bf16[512,1024]{1,0:T(8,128)(2,1)S(1)}, u32[]{:S(2)}, u32[]{:S(2)}) collective-permute-start(bf16[512,1024]{1,0:T(8,128)(2,1)S(1)} %get-tuple-element.60), channel_id=1, source_target_pairs={{0,2},{1,5},{2,0},{3,7},{4,6},{5,1},{6,4},{7,3},{8,10},{9,13},{10,... | collective-permute-start | bytes 3145736 | tf_op jit(solution)/shard_map/ppermute | solution.py:263
  15.7 8.0 %copy-start.3 = (bf16[512,1024]{1,0:T(8,128)(2,1)}, bf16[512,1024]{1,0:T(8,128)(2,1)S(1)}, u32[]{:S(2)}) copy-start(bf16[512,1024]{1,0:T(8,128)(2,1)S(1)} %collective-permute-done.3) | copy-start | bytes 3145732
  18.8 66.6 %collective-permute-start.4 = (bf16[1024,1024]{1,0:T(8,128)(2,1)}, bf16[1024,1024]{1,0:T(8,128)(2,1)}, u32[]{:S(2)}, u32[]{:S(2)}) collective-permute-start(bf16[1024,1024]{1,0:T(8,128)(2,1)} %pad_maximum_fusion.4), channel_id=1, source_target_pairs={{0,4},{1,3},{2,6},{3,1},{4,0},{5,7},{6,2},{7,5},{8,12},{9,11},{10,... | collective-permute-start | bytes 6291464 | tf_op jit(solution)/shard_map/ppermute | solution.py:263
  22.6 12.7 %copy-start.12 = (bf16[8,32,384]{2,1,0:T(8,128)(2,1)S(1)}, bf16[8,32,384]{2,1,0:T(8,128)(2,1)}, u32[]{:S(2)}) copy-start(bf16[8,32,384]{2,1,0:T(8,128)(2,1)} %reshape.773) | copy-start | bytes 589828
  28.8 13.1 %copy-start.20 = (bf16[32,1024]{1,0:T(8,128)(2,1)S(1)}, bf16[32,1024]{1,0:T(8,128)(2,1)}, u32[]{:S(2)}) copy-start(bf16[32,1024]{1,0:T(8,128)(2,1)} %param.19) | copy-start | bytes 196612
  34.7 54.3 %collective-permute-start.1 = (bf16[1024,1024]{1,0:T(8,128)(2,1)}, bf16[1024,1024]{1,0:T(8,128)(2,1)}, u32[]{:S(2)}, u32[]{:S(2)}) collective-permute-start(bf16[1024,1024]{1,0:T(8,128)(2,1)} %pad_maximum_fusion.3), channel_id=1, source_target_pairs={{0,4},{1,3},{2,6},{3,1},{4,0},{5,7},{6,2},{7,5},{8,12},{9,11},{10,... | collective-permute-start | bytes 6291464 | tf_op jit(solution)/shard_map/ppermute | solution.py:263
  36.2 48.2 %copy-start = (bf16[512,1024]{1,0:T(8,128)(2,1)S(1)}, bf16[512,1024]{1,0:T(8,128)(2,1)}, u32[]{:S(2)}) copy-start(bf16[512,1024]{1,0:T(8,128)(2,1)} %param.15) | copy-start | bytes 3145732
  36.2 41.4 %all-to-all-start = ((bf16[8,32,1024]{2,1,0:T(8,128)(2,1)}), bf16[8,32,1024]{2,1,0:T(8,128)(2,1)}, u32[]{:S(2)}, u32[]{:S(2)}) async-start(bf16[8,32,1024]{2,1,0:T(8,128)(2,1)} %pad_maximum_fusion.6), calls=%async_computation | async-start | bytes 1048576 | tf_op jit(solution)/shard_map/all_to_all | solution.py:279
  78.8 32.3 %all-to-all-start.3 = ((bf16[4,160,1024]{2,1,0:T(8,128)(2,1)}), bf16[4,160,1024]{2,1,0:T(8,128)(2,1)}, u32[]{:S(2)}, u32[]{:S(2)}) async-start(bf16[4,160,1024]{2,1,0:T(8,128)(2,1)} %broadcast_in_dim.149), calls=%async_computation.3 | async-start | bytes 2621440 | tf_op jit(solution)/shard_map/all_to_all | solution.py:279
  89.0 77.6 %collective-permute-start.5 = (bf16[2048,1024]{1,0:T(8,128)(2,1)}, bf16[2048,1024]{1,0:T(8,128)(2,1)}, u32[]{:S(2)}, u32[]{:S(2)}) collective-permute-start(bf16[2048,1024]{1,0:T(8,128)(2,1)} %pad_maximum_fusion.2), channel_id=1, source_target_pairs={{0,1},{1,0},{2,3},{3,2},{4,5},{5,4},{6,7},{7,6},{8,9},{9,8},{10,11... | collective-permute-start | bytes 12582920 | tf_op jit(solution)/shard_map/ppermute | solution.py:263
  92.6 94.4 %collective-permute-start.2 = (bf16[2048,1024]{1,0:T(8,128)(2,1)}, bf16[2048,1024]{1,0:T(8,128)(2,1)}, u32[]{:S(2)}, u32[]{:S(2)}) collective-permute-start(bf16[2048,1024]{1,0:T(8,128)(2,1)} %pad_maximum_fusion.1), channel_id=1, source_target_pairs={{0,1},{1,0},{2,3},{3,2},{4,5},{5,4},{6,7},{7,6},{8,9},{9,8},{10,11... | collective-permute-start | bytes 12582920 | tf_op jit(solution)/shard_map/ppermute | solution.py:263
  112.3 35.2 %all-to-all-start.2 = ((bf16[4,256,640]{2,1,0:T(8,128)(2,1)}), bf16[4,256,640]{2,1,0:T(8,128)(2,1)}, u32[]{:S(2)}, u32[]{:S(2)}) async-start(bf16[4,256,640]{2,1,0:T(8,128)(2,1)} %broadcast_in_dim.131), calls=%async_computation.2 | async-start | bytes 2621440 | tf_op jit(solution)/shard_map/all_to_all | solution.py:279
  122.1 11.2 %copy-start.4 = (bf16[512,1024]{1,0:T(8,128)(2,1)S(1)}, bf16[512,1024]{1,0:T(8,128)(2,1)}, u32[]{:S(2)}) copy-start(bf16[512,1024]{1,0:T(8,128)(2,1)} %copy-done.3) | copy-start | bytes 3145732
  132.2 15.4 %copy-start.13 = (bf16[256,384]{1,0:T(8,128)(2,1)S(1)}, bf16[256,384]{1,0:T(8,128)(2,1)}, u32[]{:S(2)}) copy-start(bf16[256,384]{1,0:T(8,128)(2,1)} %slice.160) | copy-start | bytes 589828
  133.2 3.4 collective-permute-start.6
  148.5 81.8 %all-to-all-start.1 = ((bf16[4,256,384]{2,1,0:T(8,128)(2,1)}), bf16[4,256,384]{2,1,0:T(8,128)(2,1)}, u32[]{:S(2)}, u32[]{:S(2)}) async-start(bf16[4,256,384]{2,1,0:T(8,128)(2,1)} %broadcast_in_dim.130), calls=%async_computation.1 | async-start | bytes 1572864 | tf_op jit(solution)/shard_map/all_to_all | solution.py:279
  293.2 6.2 %copy-start.5 = (bf16[4096,1024]{1,0:T(8,128)(2,1)S(1)}, bf16[4096,1024]{1,0:T(8,128)(2,1)}, u32[]{:S(2)}) copy-start(bf16[4096,1024]{1,0:T(8,128)(2,1)} %get-tuple-element.40) | copy-start | bytes 25165828
  298.2 50.5 %collective-permute-start.10 = (bf16[2048,1024]{1,0:T(8,128)(2,1)}, bf16[2048,1024]{1,0:T(8,128)(2,1)}, u32[]{:S(2)}, u32[]{:S(2)}) collective-permute-start(bf16[2048,1024]{1,0:T(8,128)(2,1)} %slice.143), channel_id=1, source_target_pairs={{0,1},{1,0},{2,3},{3,2},{4,5},{5,4},{6,7},{7,6},{8,9},{9,8},{10,11... | collective-permute-start | bytes 12582920 | tf_op jit(solution)/shard_map/ppermute | solution.py:263
  299.4 2.6 copy-start.17
  299.4 2.9 copy-start.16
  299.4 3.2 copy-start.15
  299.4 3.5 copy-start.14
  299.4 3.8 copy-start.24
  299.4 4.1 copy-start.23
  301.9 17.2 %copy-start.18 = (bf16[128,1024]{1,0:T(8,128)(2,1)S(1)}, bf16[128,1024]{1,0:T(8,128)(2,1)}, u32[]{:S(2)}) copy-start(bf16[128,1024]{1,0:T(8,128)(2,1)} %get-tuple-element.43) | copy-start | bytes 786436
  301.9 55.4 %collective-permute-start.7 = (bf16[2048,1024]{1,0:T(8,128)(2,1)}, bf16[2048,1024]{1,0:T(8,128)(2,1)}, u32[]{:S(2)}, u32[]{:S(2)}) collective-permute-start(bf16[2048,1024]{1,0:T(8,128)(2,1)} %slice.135), channel_id=1, source_target_pairs={{0,1},{1,0},{2,3},{3,2},{4,5},{5,4},{6,7},{7,6},{8,9},{9,8},{10,11... | collective-permute-start | bytes 12582920 | tf_op jit(solution)/shard_map/ppermute | solution.py:263
  314.2 27.8 %all-to-all-start.6 = ((bf16[4,256,512]{2,1,0:T(8,128)(2,1)}), bf16[4,256,512]{2,1,0:T(8,128)(2,1)S(1)}, u32[]{:S(2)}, u32[]{:S(2)}) async-start(bf16[4,256,512]{2,1,0:T(8,128)(2,1)} %bitcast.42), calls=%async_computation.6 | async-start | bytes 2097152 | tf_op jit(solution)/shard_map/all_to_all | solution.py:279
  319.1 1.4 collective-permute-start.13
  341.9 12.3 %copy-start.8 = (bf16[4,256,512]{2,1,0:T(8,128)(2,1)}, bf16[4,256,512]{2,1,0:T(8,128)(2,1)S(1)}, u32[]{:S(2)}) copy-start(bf16[4,256,512]{2,1,0:T(8,128)(2,1)S(1)} %all-to-all-done.6) | copy-start | bytes 3145732
  341.9 28.8 %all-to-all-start.4 = ((bf16[4,256,512]{2,1,0:T(8,128)(2,1)}), bf16[4,256,512]{2,1,0:T(8,128)(2,1)S(1)}, u32[]{:S(2)}, u32[]{:S(2)}) async-start(bf16[4,256,512]{2,1,0:T(8,128)(2,1)} %pad_maximum_fusion.5), calls=%async_computation.4 | async-start | bytes 2097152 | tf_op jit(solution)/shard_map/all_to_all | solution.py:279
  354.3 3.0 copy-start.2
  356.0 26.4 %collective-permute-start.11 = (bf16[1024,1024]{1,0:T(8,128)(2,1)}, bf16[1024,1024]{1,0:T(8,128)(2,1)}, u32[]{:S(2)}, u32[]{:S(2)}) collective-permute-start(bf16[1024,1024]{1,0:T(8,128)(2,1)} %slice.182), channel_id=1, source_target_pairs={{0,4},{1,3},{2,6},{3,1},{4,0},{5,7},{6,2},{7,5},{8,12},{9,11},{10,... | collective-permute-start | bytes 6291464 | tf_op jit(solution)/shard_map/ppermute | solution.py:263
  362.9 2.0 copy-start.1
  366.4 51.8 %collective-permute-start.8 = (bf16[1024,1024]{1,0:T(8,128)(2,1)}, bf16[1024,1024]{1,0:T(8,128)(2,1)}, u32[]{:S(2)}, u32[]{:S(2)}) collective-permute-start(bf16[1024,1024]{1,0:T(8,128)(2,1)} %slice.176), channel_id=1, source_target_pairs={{0,4},{1,3},{2,6},{3,1},{4,0},{5,7},{6,2},{7,5},{8,12},{9,11},{10,... | collective-permute-start | bytes 6291464 | tf_op jit(solution)/shard_map/ppermute | solution.py:263
  370.7 8.3 %copy-start.9 = (bf16[4,256,512]{2,1,0:T(8,128)(2,1)}, bf16[4,256,512]{2,1,0:T(8,128)(2,1)S(1)}, u32[]{:S(2)}) copy-start(bf16[4,256,512]{2,1,0:T(8,128)(2,1)S(1)} %all-to-all-done.4) | copy-start | bytes 3145732
  370.8 29.4 %all-to-all-start.8 = ((bf16[4,128,1024]{2,1,0:T(8,128)(2,1)}), bf16[4,128,1024]{2,1,0:T(8,128)(2,1)}, u32[]{:S(2)}, u32[]{:S(2)}) async-start(bf16[4,128,1024]{2,1,0:T(8,128)(2,1)} %bitcast.45), calls=%async_computation.8 | async-start | bytes 2097152 | tf_op jit(solution)/shard_map/all_to_all | solution.py:279
  379.0 9.0 %copy-start.21 = (f32[3,128]{1,0:T(4,128)}, f32[3,128]{1,0:T(4,128)S(1)}, u32[]{:S(2)}) copy-start(f32[3,128]{1,0:T(4,128)S(1)} %reduce_sum.92) | copy-start | bytes 4612
  386.6 62.2 %collective-permute-start.12 = (bf16[512,1024]{1,0:T(8,128)(2,1)}, bf16[512,1024]{1,0:T(8,128)(2,1)}, u32[]{:S(2)}, u32[]{:S(2)}) collective-permute-start(bf16[512,1024]{1,0:T(8,128)(2,1)} %slice.184), channel_id=1, source_target_pairs={{0,2},{1,5},{2,0},{3,7},{4,6},{5,1},{6,4},{7,3},{8,10},{9,13},{10,... | collective-permute-start | bytes 3145736 | tf_op jit(solution)/shard_map/ppermute | solution.py:263
  392.1 0.8 copy-start.11
  400.2 24.9 %all-to-all-start.7 = ((bf16[8,32,512]{2,1,0:T(8,128)(2,1)}), bf16[8,32,512]{2,1,0:T(8,128)(2,1)S(1)}, u32[]{:S(2)}, u32[]{:S(2)}) async-start(bf16[8,32,512]{2,1,0:T(8,128)(2,1)} %bitcast.116), calls=%async_computation.7 | async-start | bytes 524288 | tf_op jit(solution)/shard_map/all_to_all | solution.py:279
  421.3 1.3 copy-start.6
  422.7 12.4 %slice-start = ((f32[256,512]{1,0:T(8,128)}), f32[256,128]{1,0:T(8,128)S(1)}, s32[]{:S(2)}) async-start(f32[256,512]{1,0:T(8,128)} %copy-done.11), calls=%async_computation.10 | async-start | bytes 262144 | tf_op jit(solution)/shard_map/slice | solution.py:718
  423.7 27.2 %collective-permute-start.9 = (bf16[512,1024]{1,0:T(8,128)(2,1)}, bf16[512,1024]{1,0:T(8,128)(2,1)}, u32[]{:S(2)}, u32[]{:S(2)}) collective-permute-start(bf16[512,1024]{1,0:T(8,128)(2,1)} %slice.178), channel_id=1, source_target_pairs={{0,2},{1,5},{2,0},{3,7},{4,6},{5,1},{6,4},{7,3},{8,10},{9,13},{10,... | collective-permute-start | bytes 3145736 | tf_op jit(solution)/shard_map/ppermute | solution.py:263
  425.1 16.3 %all-to-all-start.5 = ((bf16[8,32,384]{2,1,0:T(8,128)(2,1)}), bf16[8,32,384]{2,1,0:T(8,128)(2,1)}, u32[]{:S(2)}, u32[]{:S(2)}) async-start(bf16[8,32,384]{2,1,0:T(8,128)(2,1)} %bitcast.125), calls=%async_computation.5 | async-start | bytes 393216 | tf_op jit(solution)/shard_map/all_to_all | solution.py:279
  448.8 2.2 copy-start.7
  448.8 2.2 copy-start.10
  450.9 3.8 copy-start.26
